TPU v7x, 512 devices: a whole 4x4x16 slice. The times are simulated.
512 devices in a mesh: elem: 32 (over z_lo, x), mode: 16 (over z_hi, y, core).
Axes of the slice: x: 4, y: 4, z: 16 (z_hi: 2, z_lo: 8; z = z_hi * 8 + z_lo), core: 2. Of those that a mesh axis runs over, the one named last changes fastest.
Arguments:
- displacement: float32 [2, 3, 512, 18432], P(None, None, 'mode', 'elem'), may hold values from -0.01171875 to 0.01171875
- metric: float32 [4, 18432], P(None, 'elem'), may hold values from -4 to 4
- weight_jac: float32 [18432], P('elem'), may hold values from 0.2 to 2
- radius: float32 [18432], P('elem'), may hold values from 0.5 to 2
- moduli: float32 [2, 512], P(None, 'elem'), may hold values from 0.5 to 4
- neighbours: int32 [512, 2], P('elem'), may hold values from -1 to 511, as said below
- inner_side: int32 [512], P('elem'), may hold values 0 or 1
- pressure: float32 [512], P('mode'), may hold values from -0.3 to 0.3
Outputs:
- residual: float32 [2, 3, 512, 18432], P(None, None, 'mode', 'elem')
Inputs may be any that keep to these rules, and one draw needn't show every extreme that they name: The elements form one chain. neighbours[e, 0] is the element across the eta = -1 face of e and neighbours[e, 1] the element across its eta = +1 face, -1 at the chain's two ends; node (a, 0) of an element meets node (a, 5) of the element before it. The 16 elements of each index of elem form one run of the chain, stored in any order, and the runs follow the indices of elem in order.
All inputs are finite; a program needn't handle non-finite values. No bound on the sum of `inner_side` on one device may be relied on, other than what follows from the above.
Results may differ from a plain program's by a relative error of at most 0.00015.
Values sent between devices are 32-bit elements; how exact they have to be, the bound alone decides.
A program may use at most 64 MiB of HBM per device.

v0:
```python
import math

import jax
import jax.numpy as jnp
import ml_dtypes
import numpy as np
from jax import lax
from jax.experimental import pallas as pl
from jax.experimental.pallas import tpu as pltpu
from jax.sharding import PartitionSpec as P

MODES = 256
ANGLES = 512
COEFS = 512
NODES = 36
PEERS = 16
OWN = 32
POINTS = 576
WIDE = 640
BLOCK = 128
MESH = pl.DeviceIdType.MESH
f32, bf16 = jnp.float32, jnp.bfloat16

OFFSETS = [(dz, dy, dc) for dz in (1, 0) for dy in (2, 1, 3, 0) for dc in (1, 0) if dz + dy + dc]


def line_derivative():
    inner_node = math.sqrt(1.0 / 3.0 - 2.0 * math.sqrt(7.0) / 21.0)
    outer_node = math.sqrt(1.0 / 3.0 + 2.0 * math.sqrt(7.0) / 21.0)
    gll_nodes = np.array([-1.0, -outer_node, -inner_node, inner_node, outer_node, 1.0])
    weights = np.array(
        [1.0 / np.prod([gll_nodes[j] - gll_nodes[k] for k in range(6) if k != j]) for j in range(6)]
    )
    derivative = np.zeros((6, 6))
    for i in range(6):
        for j in range(6):
            if i != j:
                derivative[i, j] = weights[j] / weights[i] / (gll_nodes[i] - gll_nodes[j])
        derivative[i, i] = -np.sum(derivative[i])
    return derivative


def halves(table):
    high = table.astype(np.float32).astype(ml_dtypes.bfloat16)
    low = (table - high.astype(np.float64)).astype(np.float32).astype(ml_dtypes.bfloat16)
    return high, low


def tables():
    counts = np.arange(ANGLES)
    orders = np.arange(MODES)
    phases = (counts[:, None] * orders[None, :] % ANGLES) * (2.0 * math.pi / ANGLES)
    basis = np.zeros((ANGLES, COEFS))
    basis[:, 0::2] = np.cos(phases)
    basis[:, 1::2] = np.sin(phases)
    basis[:, 1] = np.where(counts % 2 == 0, 1.0, -1.0)
    turned = np.zeros((ANGLES, COEFS))
    turned[:, 1::2] = orders * basis[:, 0::2]
    turned[:, 0::2] = -orders * basis[:, 1::2]
    both = np.concatenate([basis, turned], axis=0)
    forward = halves(both)
    backward = halves(both.T * (2.0 * math.pi / ANGLES))
    derivative = line_derivative()
    along_xi = np.kron(derivative, np.eye(6))
    along_eta = np.kron(np.eye(6), derivative)
    spread = np.zeros((128, 768))
    for c in range(3):
        rows = slice(NODES * c, NODES * c + NODES)
        spread[rows, 128 * c : 128 * c + NODES] = along_xi.T
        spread[rows, 384 + 128 * c : 384 + 128 * c + NODES] = along_eta.T
    lanes = np.full((8, WIDE), -1, np.int32)
    points = np.arange(POINTS)
    lanes[0, :POINTS] = points // NODES
    lanes[1, :POINTS] = points % NODES // 6
    lanes[2, :POINTS] = points % 6
    lanes[3, :72] = np.arange(72) % 6
    lanes[4, :72] = np.arange(72) // 6
    return forward, backward, halves(spread), halves(spread.T), lanes


def split(values):
    high = values.astype(bf16)
    return high, (values - high.astype(f32)).astype(bf16)


def dot(a, b):
    return jnp.dot(a, b, preferred_element_type=f32)


def turn(values, shift):
    shift = shift % 128
    return pltpu.roll(values, shift, 1) if shift else values


def kernel(
    disp, geo, pres, lanes, neigh, side, moduli,
    fwd_hi, fwd_lo, bwd_hi, bwd_lo, der_hi, der_lo, ted_hi, ted_lo,
    out,
    pack, got1, got2, state1, fields, back0, back1, home0, home1, perm, rims, rim_out, rim_in, base,
    tfh, tfl, tbh, tbl, tdh, tdl, teh, tel,
    table_sem, send1, recv1, send2, recv2, send3, recv3, send4, recv4, rim_send, rim_recv,
):
    elem = lax.axis_index("elem")
    mode = lax.axis_index("mode")
    runs = lax.axis_size("elem")
    half, rest = mode // 8, mode % 8
    row, core = rest // 2, rest % 2

    def peer(dz, dy, dc):
        return (half + dz + 2) % 2 * 8 + (row + dy + 4) % 4 * 2 + (core + dc + 2) % 2

    barrier = pltpu.get_barrier_semaphore()
    for dz, dy, dc in OFFSETS:
        pl.semaphore_signal(barrier, inc=1, device_id=(elem, peer(-dz, -dy, -dc)), device_id_type=MESH)

    @pl.when(elem > 0)
    def _():
        pl.semaphore_signal(barrier, inc=1, device_id=(elem - 1, mode), device_id_type=MESH)

    @pl.when(elem < runs - 1)
    def _():
        pl.semaphore_signal(barrier, inc=1, device_id=(elem + 1, mode), device_id_type=MESH)

    table_copies = []
    for i, (src, dst) in enumerate(
        [(fwd_hi, tfh), (fwd_lo, tfl), (der_hi, tdh), (der_lo, tdl), (ted_hi, teh), (ted_lo, tel),
         (bwd_hi, tbh), (bwd_lo, tbl)]
    ):
        copy = pltpu.make_async_copy(src, dst, table_sem.at[i])
        copy.start()
        table_copies.append(copy)

    lane = lax.broadcasted_iota(jnp.int32, (OWN, 128), 1)
    lane8 = lax.broadcasted_iota(jnp.int32, (8, 128), 1)

    def column(s, c, g):
        if g < 4:
            return disp[s, c, :, 128 * g : 128 * g + 128]
        return jnp.concatenate([disp[s, c, :, 512:576], jnp.zeros((OWN, 64), f32)], axis=1)

    def gather_element(s, j, base_lane):
        result = jnp.zeros((OWN, 128), f32)
        for c in range(3):
            target = NODES * c + base_lane
            first = NODES * j
            for g in range(first // 128, (first + NODES - 1) // 128 + 1):
                low = max(first, 128 * g)
                high = min(first + NODES, 128 * g + 128)
                moved = turn(column(s, c, g), target - (first - 128 * g))
                begin = (target + low - first) % 128
                end = begin + high - low
                inside = (lane >= begin) & (lane < end)
                if end > 128:
                    inside = (lane >= begin) | (lane < end - 128)
                result = jnp.where(inside, moved, result)
        return result

    def pack_rows(full, ragged):
        last = ragged[24:32]
        tails = [turn(last, 88), turn(last, 48), turn(last, 8)]
        rows = [jnp.where(lane8 < 88, ragged[8 * t : 8 * t + 8], tails[t]) for t in range(3)]
        return jnp.where(lane < 108, full, ragged), jnp.concatenate(rows, axis=0)

    def unpack_ragged(first, second):
        rows = [
            jnp.where(lane8 < 88, second[8 * t : 8 * t + 8], first[8 * t : 8 * t + 8]) for t in range(3)
        ]
        moved = [turn(second[0:8], -88), turn(second[8:16], -48), turn(second[16:24], -8)]
        last = jnp.where(lane8 < 40, moved[0], jnp.where(lane8 < 80, moved[1], moved[2]))
        rows.append(jnp.where(lane8 < 88, last, first[24:32]))
        return jnp.concatenate(rows, axis=0)

    for j in range(PEERS):
        full = gather_element(0, j, 0)
        ragged = gather_element(1, j, 108)
        top, bottom = pack_rows(full, ragged)
        pack[j, 0:32, :] = top
        pack[j, 32:56, :] = bottom

    neighbours_there = 2 - (elem == 0).astype(jnp.int32) - (elem == runs - 1).astype(jnp.int32)
    pl.semaphore_wait(barrier, len(OFFSETS) + neighbours_there)

    def exchange(source, target, send, recv):
        copies = []
        for i, (dz, dy, dc) in enumerate(OFFSETS):
            to = peer(dz, dy, dc)
            copy = pltpu.make_async_remote_copy(
                src_ref=source(to),
                dst_ref=target.at[mode],
                send_sem=send.at[i],
                recv_sem=recv.at[i],
                device_id=(elem, to),
                device_id_type=MESH,
            )
            copy.start()
            copies.append(copy)
        return copies

    there1 = exchange(lambda to: pack.at[to, 0:32], got1, send1, recv1)
    there2 = exchange(lambda to: pack.at[to, 32:56], got2, send2, recv2)
    got1[mode] = pack[mode, 0:32, :]
    got2[mode] = pack[mode, 32:56, :]

    def own_row(i):
        moved = pltpu.roll(geo[...], (WIDE - NODES * mode) % WIDE, 1)
        return moved[i : i + 1, 0:128]

    lane1 = lax.broadcasted_iota(jnp.int32, (1, 128), 1)
    real = lane1 < NODES
    xi_r, xi_z, eta_r, eta_z, weight, radius = [jnp.where(real, own_row(i), 0.0) for i in range(6)]
    radius = jnp.where(real, radius, 1.0)
    rho = 1.0 / radius
    shear = moduli[0, mode]
    bulk = moduli[1, mode]
    scale = weight * radius
    back_rows = [scale * xi_r, scale * xi_z, scale * eta_r, scale * eta_z]

    first_elem = elem * PEERS
    head = jnp.int32(0)
    tail = jnp.int32(0)
    e_lane, a_lane, b_lane = lanes[0:1, :], lanes[1:2, :], lanes[2:3, :]
    partner = jnp.full((1, WIDE), -1, jnp.int32)
    sides = jnp.zeros((1, WIDE), jnp.int32)
    for e in range(PEERS):
        prev = neigh[e, 0] - first_elem
        nxt = neigh[e, 1] - first_elem
        prev_here = (prev >= 0) & (prev < PEERS)
        next_here = (nxt >= 0) & (nxt < PEERS)
        head = head + jnp.where(prev_here, 0, e)
        tail = tail + jnp.where(next_here, 0, e)
        low = jnp.where(prev_here, prev * NODES + 5, -10000)
        high = jnp.where(next_here, nxt * NODES, -10000)
        here = e_lane == e
        partner = jnp.where(here & (b_lane == 0), low + 6 * a_lane, partner)
        partner = jnp.where(here & (b_lane == 5), high + 6 * a_lane, partner)
        sides = jnp.where(here, side[e], sides)
    for g in range(5):
        rows = lax.broadcasted_iota(jnp.int32, (128, WIDE), 0) + 128 * g
        perm[128 * g : 128 * g + 128, :] = jnp.where(rows == partner, 1.0, 0.0).astype(bf16)
    node = lanes[3:4, 0:128]
    head_node = jnp.where(node >= 0, head * NODES + 6 * node, -1)
    tail_node = jnp.where(node >= 0, tail * NODES + 6 * node + 5, -1)
    for g in range(5):
        rows = lax.broadcasted_iota(jnp.int32, (128, 128), 0) + 128 * g
        rims[128 * g : 128 * g + 128, 0:128] = jnp.where(rows == head_node, 1.0, 0.0).astype(bf16)
        rims[128 * g : 128 * g + 128, 128:256] = jnp.where(rows == tail_node, 1.0, 0.0).astype(bf16)
    facing = (a_lane == 5 * sides) & (e_lane >= 0)
    outward = (2 * sides - 1).astype(f32)
    face = jnp.where(facing, 15.0 * outward * geo[4:5, :] * geo[5:6, :], 0.0)
    pressure = pres[...]
    base[0] = pressure * (face * geo[0:1, :])
    base[1] = pressure * (face * geo[1:2, :])

    for copy in table_copies:
        copy.wait()

    def evaluate(coefs, result_block):
        hi, lo = split(coefs)
        both = jnp.concatenate([hi, lo], axis=1)

        def to_angles(first):
            rows = pl.ds(pl.multiple_of(first, BLOCK), BLOCK)
            wide = dot(tfh[rows, :], both)
            return wide[:, 0:128] + wide[:, 128:256] + dot(tfl[rows, :], hi)

        def one_block(k, _):
            u = to_angles(k * BLOCK)
            r = to_angles(ANGLES + k * BLOCK)
            u_hi, u_lo = split(u)
            grads = dot(u_hi, tdh[...]) + dot(u_lo, tdh[...]) + dot(u_hi, tdl[...])
            v = [None] * 9
            for c in range(3):
                ax = grads[:, 128 * c : 128 * c + 128]
                ae = grads[:, 384 + 128 * c : 512 + 128 * c]
                v[c] = xi_r * ax + eta_r * ae
                v[3 + c] = xi_z * ax + eta_z * ae
            v[6] = r - turn(u, -NODES)
            v[7] = turn(r, -NODES) + u
            v[8] = turn(r, -2 * NODES)
            deform = [
                [1.0 + v[0], rho * v[6], v[3]],
                [v[1], 1.0 + rho * v[7], v[4]],
                [v[2], rho * v[8], 1.0 + v[5]],
            ]
            cof = [
                [
                    deform[(i + 1) % 3][(j + 1) % 3] * deform[(i + 2) % 3][(j + 2) % 3]
                    - deform[(i + 1) % 3][(j + 2) % 3] * deform[(i + 2) % 3][(j + 1) % 3]
                    for j in range(3)
                ]
                for i in range(3)
            ]
            volume = deform[0][0] * cof[0][0] + deform[0][1] * cof[0][1] + deform[0][2] * cof[0][2]
            factor = bulk * (volume - 1.0) - shear
            piola = [
                [shear * deform[i][j] + factor * cof[i][j] for j in range(3)] for i in range(3)
            ]
            parts = [back_rows[0] * piola[c][0] + back_rows[1] * piola[c][2] for c in range(3)]
            parts += [back_rows[2] * piola[c][0] + back_rows[3] * piola[c][2] for c in range(3)]
            p_hi, p_lo = split(jnp.concatenate(parts, axis=1))
            hoop = [weight * piola[c][1] for c in range(3)]
            straight = dot(p_hi, teh[...]) + dot(p_lo, teh[...]) + dot(p_hi, tel[...])
            straight = straight + hoop[1] - turn(hoop[0], NODES)
            turned = hoop[0] + turn(hoop[1], NODES) + turn(hoop[2], 2 * NODES)
            for start, value in ((0, straight), (ANGLES, turned)):
                v_hi, v_lo = split(value)
                rows = pl.ds(pl.multiple_of(start + k * BLOCK, BLOCK), BLOCK)
                fields[rows, 0:128] = v_hi
                fields[rows, 128:256] = v_lo
            return 0

        lax.fori_loop(0, ANGLES // BLOCK, one_block, 0)

        def back_block(k, _):
            rows = pl.ds(pl.multiple_of(k * BLOCK, BLOCK), BLOCK)
            wide = dot(tbh[rows, :], fields[...])
            result_block(k, wide[:, 0:128] + wide[:, 128:256] + dot(tbl[rows, :], fields[:, 0:128]))
            return 0

        lax.fori_loop(0, COEFS // BLOCK, back_block, 0)

    for copy in there1:
        copy.wait_recv()

    def keep_ragged(k, block):
        block = turn(block, 108)
        for q in range(BLOCK // OWN):
            _, bottom = pack_rows(block[OWN * q : OWN * q + OWN], block[OWN * q : OWN * q + OWN])
            back0[k * (BLOCK // OWN) + q] = bottom
            back1[k * (BLOCK // OWN) + q] = block[OWN * q : OWN * q + OWN]

    evaluate(got1[...].reshape(COEFS, 128), keep_ragged)
    again0 = exchange(lambda to: back0.at[to], home0, send3, recv3)
    home0[mode] = back0[mode]

    for copy in there2:
        copy.wait_recv()
    for i in range(PEERS):
        state1[OWN * i : OWN * i + OWN, :] = turn(unpack_ragged(got1[i], got2[i]), 20)

    def keep_full(k, block):
        for q in range(BLOCK // OWN):
            i = k * (BLOCK // OWN) + q
            back1[i] = jnp.where(lane < 108, block[OWN * q : OWN * q + OWN], back1[i])

    evaluate(state1[...], keep_full)
    again1 = exchange(lambda to: back1.at[to], home1, send4, recv4)
    home1[mode] = back1[mode]

    for copy in again0 + again1:
        copy.wait_recv()

    pieces = [[turn(unpack_ragged(home1[i], home0[i]), 20) for i in range(PEERS)],
              [home1[i] for i in range(PEERS)]]
    loaded = []
    for s in range(2):
        for c in range(3):
            columns = []
            for g in range(5):
                acc = jnp.zeros((OWN, 128), f32)
                for i in range(PEERS):
                    low = max(NODES * i, 128 * g) - 128 * g
                    high = min(NODES * i + NODES, 128 * g + 128) - 128 * g
                    if low < high:
                        moved = turn(pieces[s][i], NODES * i - 128 * g - NODES * c)
                        acc = jnp.where((lane >= low) & (lane < high), moved, acc)
                columns.append(acc)
            whole = jnp.concatenate(columns, axis=1)
            if c == 0:
                whole = whole + base[0]
            elif c == 2:
                whole = whole + base[1]
            loaded.append(whole)
    loaded = jnp.concatenate(loaded, axis=0)
    l_hi, l_lo = split(loaded)

    traces = dot(l_hi, rims[...]) + dot(l_lo, rims[...])
    slot = lanes[4:5, 0:128]
    for way in range(2):
        trace = traces[:, 128 * way : 128 * way + 128]
        for s in range(2):
            tile = jnp.zeros((8, 128), f32)
            for t in range(12):
                tile = jnp.where(slot == t, trace[96 * s + 8 * t : 96 * s + 8 * t + 8], tile)
            rim_out[way, 8 * s : 8 * s + 8, :] = tile

    to_prev = pltpu.make_async_remote_copy(
        src_ref=rim_out.at[0], dst_ref=rim_in.at[1], send_sem=rim_send.at[0], recv_sem=rim_recv.at[1],
        device_id=(jnp.maximum(elem - 1, 0), mode), device_id_type=MESH,
    )
    to_next = pltpu.make_async_remote_copy(
        src_ref=rim_out.at[1], dst_ref=rim_in.at[0], send_sem=rim_send.at[1], recv_sem=rim_recv.at[0],
        device_id=(jnp.minimum(elem + 1, runs - 1), mode), device_id_type=MESH,
    )

    @pl.when(elem > 0)
    def _():
        to_prev.start()

    @pl.when(elem < runs - 1)
    def _():
        to_next.start()

    result = loaded + dot(l_hi, perm[...]) + dot(l_lo, perm[...])

    @pl.when(elem > 0)
    def _():
        to_next.wait_recv()

    @pl.when(elem < runs - 1)
    def _():
        to_prev.wait_recv()

    arrived = []
    for way, there in ((0, elem > 0), (1, elem < runs - 1)):
        rows = []
        for s in range(2):
            tile = jnp.where(there, rim_in[way, 8 * s : 8 * s + 8, :], 0.0)
            rows += [jnp.where(slot == t, tile, 0.0) for t in range(12)]
        arrived.append(jnp.concatenate(rows, axis=0))
    a_hi, a_lo = split(jnp.concatenate(arrived, axis=1))
    for part in (a_hi, a_lo):
        result = result + lax.dot_general(
            part, rims[...], (((1,), (1,)), ((), ())), preferred_element_type=f32
        )
    for s in range(2):
        for c in range(3):
            first = 96 * s + 32 * c
            out[s, c] = result[first : first + 32, 0:POINTS]

    for copy in there1 + there2 + again0 + again1:
        copy.wait_send()

    @pl.when(elem > 0)
    def _():
        to_prev.wait_send()

    @pl.when(elem < runs - 1)
    def _():
        to_next.wait_send()


def on_device(displacement, metric, weight_jac, radius, moduli, neighbours, inner_side, pressure):
    forward, backward, spread, gather, lanes = tables()
    geo = jnp.concatenate(
        [metric, weight_jac[None, :], radius[None, :], jnp.zeros((2, POINTS), f32)], axis=0
    )
    geo = jnp.pad(geo, ((0, 0), (0, WIDE - POINTS)))
    vmem = pl.BlockSpec(memory_space=pltpu.VMEM)
    smem = pl.BlockSpec(memory_space=pltpu.SMEM)
    anywhere = pl.BlockSpec(memory_space=pl.ANY)
    constants = [jnp.asarray(t) for t in (*forward, *backward, *spread, *gather)]
    dma = pltpu.SemaphoreType.DMA((len(OFFSETS),))
    return pl.pallas_call(
        kernel,
        out_shape=jax.ShapeDtypeStruct((2, 3, OWN, POINTS), f32),
        in_specs=[vmem] * 4 + [smem] * 3 + [anywhere] * 8,
        out_specs=vmem,
        scratch_shapes=[
            pltpu.VMEM((PEERS, 56, 128), f32),
            pltpu.VMEM((PEERS, 32, 128), f32),
            pltpu.VMEM((PEERS, 24, 128), f32),
            pltpu.VMEM((COEFS, 128), f32),
            pltpu.VMEM((2 * ANGLES, 256), bf16),
            pltpu.VMEM((PEERS, 24, 128), f32),
            pltpu.VMEM((PEERS, 32, 128), f32),
            pltpu.VMEM((PEERS, 24, 128), f32),
            pltpu.VMEM((PEERS, 32, 128), f32),
            pltpu.VMEM((WIDE, WIDE), bf16),
            pltpu.VMEM((WIDE, 256), bf16),
            pltpu.VMEM((2, 16, 128), f32),
            pltpu.VMEM((2, 16, 128), f32),
            pltpu.VMEM((2, OWN, WIDE), f32),
            pltpu.VMEM((2 * ANGLES, COEFS), bf16),
            pltpu.VMEM((2 * ANGLES, COEFS), bf16),
            pltpu.VMEM((COEFS, 2 * ANGLES), bf16),
            pltpu.VMEM((COEFS, 2 * ANGLES), bf16),
            pltpu.VMEM((128, 768), bf16),
            pltpu.VMEM((128, 768), bf16),
            pltpu.VMEM((768, 128), bf16),
            pltpu.VMEM((768, 128), bf16),
            pltpu.SemaphoreType.DMA((8,)),
            dma, dma, dma, dma, dma, dma, dma, dma,
            pltpu.SemaphoreType.DMA((2,)),
            pltpu.SemaphoreType.DMA((2,)),
        ],
        compiler_params=pltpu.CompilerParams(
            collective_id=0, has_side_effects=True, vmem_limit_bytes=48 * 2**20
        ),
        name="bellows",
    )(
        displacement, geo, pressure[:, None], jnp.asarray(lanes), neighbours, inner_side, moduli,
        *constants,
    )


def solution(mesh):
    placed = (
        P(None, None, "mode", "elem"),
        P(None, "elem"),
        P("elem"),
        P("elem"),
        P(None, "elem"),
        P("elem", None),
        P("elem"),
        P("mode"),
    )
    return jax.shard_map(
        on_device,
        mesh=mesh,
        in_specs=placed,
        out_specs=P(None, None, "mode", "elem"),
        check_vma=False,
    )
```

profile of v0, /device:TPU:64, one launch (start us, length us, event | category | flops | bytes accessed | tf_op | source)
XLA Modules:
  0.0 83.9 jit_solution(6327345056325125781)
XLA Ops:
  0.0 0.0 copy-start.13
  0.0 0.0 copy-start.14
  0.0 0.0 copy-start.15
  0.0 0.1 pad.8.clone
  0.1 0.6 copy-done.13
  0.7 0.0 copy-start.12
  0.7 0.0 copy-done.14
  0.7 0.0 copy-done.15
  0.7 0.1 copy.19.neigh
  0.8 0.6 copy-done.12
  1.4 0.1 maximum_maximum_fusion
  1.5 0.0 copy-start.16
  1.5 0.0 copy-start.9
  1.5 0.6 copy-done.16
  2.1 0.0 copy-start.10
  2.1 0.0 copy-start.11
  2.1 0.1 copy.18.pres
  2.2 0.0 copy-done.9
  2.2 0.6 copy-done.10
  2.8 0.0 copy-done.11
  2.8 0.0 copy-start
  2.8 1.2 %copy-done = bf16[512,1024]{1,0:T(8,128)(2,1)S(1)} copy-done((bf16[512,1024]{1,0:T(8,128)(2,1)S(1)}, bf16[512,1024]{1,0:T(8,128)(2,1)}, u32[]{:S(2)}) %copy-start) | copy-done | bytes 1048600
  4.0 0.0 copy-start.1
  4.0 1.2 %copy-done.1 = bf16[512,1024]{1,0:T(8,128)(2,1)S(1)} copy-done((bf16[512,1024]{1,0:T(8,128)(2,1)S(1)}, bf16[512,1024]{1,0:T(8,128)(2,1)}, u32[]{:S(2)}) %copy-start.1) | copy-done | bytes 1048600
  5.3 0.0 copy-start.2
  5.3 1.2 %copy-done.2 = bf16[1024,512]{1,0:T(8,128)(2,1)S(1)} copy-done((bf16[1024,512]{1,0:T(8,128)(2,1)S(1)}, bf16[1024,512]{1,0:T(8,128)(2,1)}, u32[]{:S(2)}) %copy-start.2) | copy-done | bytes 1048600
  6.5 0.0 copy-start.3
  6.5 1.2 %copy-done.3 = bf16[1024,512]{1,0:T(8,128)(2,1)S(1)} copy-done((bf16[1024,512]{1,0:T(8,128)(2,1)S(1)}, bf16[1024,512]{1,0:T(8,128)(2,1)}, u32[]{:S(2)}) %copy-start.3) | copy-done | bytes 1048600
  7.7 0.0 copy-start.4
  7.7 1.0 %copy-done.4 = f32[2,3,32,576]{3,2,1,0:T(8,128)S(1)} copy-done((f32[2,3,32,576]{3,2,1,0:T(8,128)S(1)}, f32[2,3,32,576]{3,2,1,0:T(8,128)}, u32[]{:S(2)}) %copy-start.4) | copy-done | bytes 442392
  8.7 0.0 copy-start.5
  8.7 0.9 %copy-done.5 = bf16[768,128]{1,0:T(8,128)(2,1)S(1)} copy-done((bf16[768,128]{1,0:T(8,128)(2,1)S(1)}, bf16[768,128]{1,0:T(8,128)(2,1)}, u32[]{:S(2)}) %copy-start.5) | copy-done | bytes 196632
  9.7 0.0 copy-start.6
  9.7 0.9 %copy-done.6 = bf16[768,128]{1,0:T(8,128)(2,1)S(1)} copy-done((bf16[768,128]{1,0:T(8,128)(2,1)S(1)}, bf16[768,128]{1,0:T(8,128)(2,1)}, u32[]{:S(2)}) %copy-start.6) | copy-done | bytes 196632
  10.6 0.0 copy-start.7
  10.6 0.9 %copy-done.7 = bf16[128,768]{1,0:T(8,128)(2,1)S(1)} copy-done((bf16[128,768]{1,0:T(8,128)(2,1)S(1)}, bf16[128,768]{1,0:T(8,128)(2,1)}, u32[]{:S(2)}) %copy-start.7) | copy-done | bytes 196632
  11.5 0.0 copy-start.8
  11.5 0.9 %copy-done.8 = bf16[128,768]{1,0:T(8,128)(2,1)S(1)} copy-done((bf16[128,768]{1,0:T(8,128)(2,1)S(1)}, bf16[128,768]{1,0:T(8,128)(2,1)}, u32[]{:S(2)}) %copy-start.8) | copy-done | bytes 196632
  12.4 70.7 %bellows.1 = f32[2,3,32,576]{3,2,1,0:T(8,128)S(1)} custom-call(f32[2,3,32,576]{3,2,1,0:T(8,128)S(1)} %copy-done.4, f32[8,640]{1,0:T(8,128)S(1)} %pad.4.geo, f32[32,1]{1,0:T(8,128)S(1)} %copy.18.pres, s32[8,640]{1,0:T(8,128)S(1)} %copy-done.9, s32[16,2]{1,0:T(8,128)S(1)} %copy.19.neigh, s32[16]{0:T(128)S(1)} %copy-done.11, f32[2,16]{1,0:T(2,128)S(1)} %copy-done.10, ...), custom_call_target="tpu_custom_call" | custom-call | tf_op jit(solution)/shard_map/bellows/pallas_call | solution.py:454
  83.1 0.8 copy.21
  (4 shorter events, 0.0 us)
Async XLA Ops:
  0.0 0.7 copy-start.13
  0.0 0.7 copy-start.14
  0.0 0.7 copy-start.15
  0.7 0.7 copy-start.12
  1.5 0.7 copy-start.16
  1.5 0.7 copy-start.9
  2.1 0.7 copy-start.10
  2.1 0.7 copy-start.11
  2.8 1.2 %copy-start = (bf16[512,1024]{1,0:T(8,128)(2,1)S(1)}, bf16[512,1024]{1,0:T(8,128)(2,1)}, u32[]{:S(2)}) copy-start(bf16[512,1024]{1,0:T(8,128)(2,1)} %constant.25.clone.bwd_lo) | copy-start | bytes 3145732
  4.0 1.2 %copy-start.1 = (bf16[512,1024]{1,0:T(8,128)(2,1)S(1)}, bf16[512,1024]{1,0:T(8,128)(2,1)}, u32[]{:S(2)}) copy-start(bf16[512,1024]{1,0:T(8,128)(2,1)} %constant.24.clone.bwd_hi) | copy-start | bytes 3145732
  5.3 1.2 %copy-start.2 = (bf16[1024,512]{1,0:T(8,128)(2,1)S(1)}, bf16[1024,512]{1,0:T(8,128)(2,1)}, u32[]{:S(2)}) copy-start(bf16[1024,512]{1,0:T(8,128)(2,1)} %constant.23.clone.fwd_lo) | copy-start | bytes 3145732
  6.5 1.2 %copy-start.3 = (bf16[1024,512]{1,0:T(8,128)(2,1)S(1)}, bf16[1024,512]{1,0:T(8,128)(2,1)}, u32[]{:S(2)}) copy-start(bf16[1024,512]{1,0:T(8,128)(2,1)} %constant.22.clone.fwd_hi) | copy-start | bytes 3145732
  7.7 1.0 %copy-start.4 = (f32[2,3,32,576]{3,2,1,0:T(8,128)S(1)}, f32[2,3,32,576]{3,2,1,0:T(8,128)}, u32[]{:S(2)}) copy-start(f32[2,3,32,576]{3,2,1,0:T(8,128)} %disp.1) | copy-start | bytes 1327108
  8.7 0.9 %copy-start.5 = (bf16[768,128]{1,0:T(8,128)(2,1)S(1)}, bf16[768,128]{1,0:T(8,128)(2,1)}, u32[]{:S(2)}) copy-start(bf16[768,128]{1,0:T(8,128)(2,1)} %constant.29.clone.ted_lo) | copy-start | bytes 589828
  9.7 0.9 %copy-start.6 = (bf16[768,128]{1,0:T(8,128)(2,1)S(1)}, bf16[768,128]{1,0:T(8,128)(2,1)}, u32[]{:S(2)}) copy-start(bf16[768,128]{1,0:T(8,128)(2,1)} %constant.28.clone.ted_hi) | copy-start | bytes 589828
  10.6 0.9 %copy-start.7 = (bf16[128,768]{1,0:T(8,128)(2,1)S(1)}, bf16[128,768]{1,0:T(8,128)(2,1)}, u32[]{:S(2)}) copy-start(bf16[128,768]{1,0:T(8,128)(2,1)} %constant.27.clone.der_lo) | copy-start | bytes 589828
  11.5 0.9 %copy-start.8 = (bf16[128,768]{1,0:T(8,128)(2,1)S(1)}, bf16[128,768]{1,0:T(8,128)(2,1)}, u32[]{:S(2)}) copy-start(bf16[128,768]{1,0:T(8,128)(2,1)} %constant.26.clone.der_hi) | copy-start | bytes 589828
where the time goes:
time: 84.5 us; the launch traced here: 83.9 us
  Pallas kernels  70.7 us (84%)
  local copies, waits for them, and re-layouts  13.1 us (16%)
    pallas_call x1, Pallas kernels, on_device(): pl.pallas_call(kernel, out_shape=jax.ShapeDtypeStruct((2, 3, OWN, POINTS)...  70.7 us
    unnamed x36, local copies, waits for them, and re-layouts  12.9 us

commit v1 on v0

v1 whole, which is shorter than its diff:
```python
import math

import jax
import jax.numpy as jnp
import ml_dtypes
import numpy as np
from jax import lax
from jax.experimental import pallas as pl
from jax.experimental.pallas import tpu as pltpu
from jax.sharding import PartitionSpec as P

MODES = 256
ANGLES = 512
COEFS = 512
NODES = 36
PEERS = 16
OWN = 32
POINTS = 576
WIDE = 640
HALF = 272
STRIP = 16
MESH = pl.DeviceIdType.MESH
f32, bf16 = jnp.float32, jnp.bfloat16

LOCAL = [(dy, dc) for dy in (2, 1, 3, 0) for dc in (1, 0) if dy + dc]
CROSS = [(dy, dc, 1 - (dy + dc) % 2 * 2) for dy in (2, 1, 3, 0) for dc in (0, 1)]
LEG = 4


def line_derivative():
    inner_node = math.sqrt(1.0 / 3.0 - 2.0 * math.sqrt(7.0) / 21.0)
    outer_node = math.sqrt(1.0 / 3.0 + 2.0 * math.sqrt(7.0) / 21.0)
    gll_nodes = np.array([-1.0, -outer_node, -inner_node, inner_node, outer_node, 1.0])
    weights = np.array(
        [1.0 / np.prod([gll_nodes[j] - gll_nodes[k] for k in range(6) if k != j]) for j in range(6)]
    )
    derivative = np.zeros((6, 6))
    for i in range(6):
        for j in range(6):
            if i != j:
                derivative[i, j] = weights[j] / weights[i] / (gll_nodes[i] - gll_nodes[j])
        derivative[i, i] = -np.sum(derivative[i])
    return derivative


def halves(table):
    high = table.astype(np.float32).astype(ml_dtypes.bfloat16)
    low = (table - high.astype(np.float64)).astype(np.float32).astype(ml_dtypes.bfloat16)
    return high, low


def tables():
    counts = np.arange(HALF)
    orders = np.arange(MODES)
    phases = (counts[:, None] * orders[None, :] % ANGLES) * (2.0 * math.pi / ANGLES)
    used = (counts <= ANGLES // 2)[:, None]
    cosines, sines = np.cos(phases) * used, np.sin(phases) * used
    from_cos = np.concatenate([cosines, -orders * sines], axis=0)
    from_sin = np.concatenate([sines, orders * cosines], axis=0)
    step = 2.0 * math.pi / ANGLES
    ends = np.where(counts == 0, 0.5, 1.0)[: ANGLES // 2, None]
    cosines, sines = step * ends * cosines[: ANGLES // 2], step * sines[: ANGLES // 2]
    to_cos = np.concatenate([cosines, -orders * sines], axis=0).T
    to_sin = np.concatenate([sines, orders * cosines], axis=0).T
    derivative = line_derivative()
    slopes = [np.kron(derivative, np.eye(6)).T, np.kron(np.eye(6), derivative).T]
    spread = np.zeros((256, 768))
    for way, slope in enumerate(slopes):
        for c in range(3):
            column = 384 * way + 128 * c
            even, odd = NODES * c, 128 + NODES * c
            spread[even : even + NODES, column : column + 2 * NODES] = np.concatenate([slope, slope], axis=1)
            spread[odd : odd + NODES, column : column + 2 * NODES] = np.concatenate([slope, -slope], axis=1)
    blocks = [from_cos, from_sin, to_cos[:, 0:256], to_cos[:, 256:512], to_sin[:, 0:256], to_sin[:, 256:512]]
    blocks += [spread[:, 0:256], spread[:, 256:512], spread[:, 512:768], spread.T]
    return np.concatenate([part for block in blocks for part in halves(block)], axis=0)


BLOCK_ROWS = [2 * HALF] * 2 + [256] * 4 + [256] * 3 + [768]
BLOCK_START = np.concatenate([[0], np.cumsum([2 * n for n in BLOCK_ROWS])]).tolist()


def split(values):
    high = values.astype(bf16)
    return high, (values - high.astype(f32)).astype(bf16)


def dot(a, b):
    return jnp.dot(a, b, preferred_element_type=f32)


def turn(values, shift):
    shift = shift % 128
    return pltpu.roll(values, shift, 1) if shift else values


def evaluate(coefs, result, rows, shear, bulk, table, scratch):
    def block(i):
        first, count = BLOCK_START[i], BLOCK_ROWS[i]
        return table[first : first + count, :], table[first + count : first + 2 * count, :]

    even_odd, turns, grads, parts, hoops, sums = scratch
    xi_r, xi_z, eta_r, eta_z, weight, radius = rows
    rho = 1.0 / radius
    scale = weight * radius
    back = [scale * xi_r, scale * xi_z, scale * eta_r, scale * eta_z]
    lane = lax.broadcasted_iota(jnp.int32, (STRIP, 128), 1)
    plus = lane < NODES

    def product(high, low, a_hi, a_lo):
        both = dot(high, jnp.concatenate([a_hi, a_lo], axis=1))
        return both[:, 0:128] + both[:, 128:256] + dot(low, a_hi)

    for order in range(2):
        both = product(*block(order), *split(coefs[pl.ds(order, MODES, stride=2), :]))
        even_odd[:, 128 * order : 128 * order + 128] = both[0:HALF]
        turns[:, 128 * order : 128 * order + 128] = both[HALF : 2 * HALF]
    sign = 1.0 - 2.0 * (lax.broadcasted_iota(jnp.int32, (HALF, 128), 0) % 2).astype(f32)
    even_odd[:, 0:128] = even_odd[:, 0:128] + sign * coefs[1:2, :]

    high, low = split(even_odd[...])
    for i in range(3):
        b_hi, b_lo = block(6 + i)
        grads[:, 256 * i : 256 * i + 256] = dot(high, b_hi) + dot(low, b_hi) + dot(high, b_lo)

    def strip(k, _):
        here = pl.ds(pl.multiple_of(k * STRIP, STRIP), STRIP)
        even, odd = even_odd[here, 0:128], even_odd[here, 128:256]
        turned_odd, turned_even = turns[here, 0:128], turns[here, 128:256]
        u_plus, u_minus = even + odd, even - odd
        r_plus, r_minus = turned_even + turned_odd, turned_even - turned_odd
        v = [None] * 9
        for c in range(3):
            ax = grads[here, 128 * c : 128 * c + 128]
            ae = grads[here, 384 + 128 * c : 512 + 128 * c]
            v[c] = xi_r * ax + eta_r * ae
            v[3 + c] = xi_z * ax + eta_z * ae
        v[6] = jnp.where(plus, r_plus - turn(u_plus, -NODES), turn(r_minus, NODES) - u_minus)
        v[7] = jnp.where(plus, turn(r_plus, -NODES) + u_plus, r_minus + turn(u_minus, NODES))
        v[8] = jnp.where(plus, turn(r_plus, -2 * NODES), turn(r_minus, -NODES))
        deform = [
            [1.0 + v[0], rho * v[6], v[3]],
            [v[1], 1.0 + rho * v[7], v[4]],
            [v[2], rho * v[8], 1.0 + v[5]],
        ]
        cof = [
            [
                deform[(i + 1) % 3][(j + 1) % 3] * deform[(i + 2) % 3][(j + 2) % 3]
                - deform[(i + 1) % 3][(j + 2) % 3] * deform[(i + 2) % 3][(j + 1) % 3]
                for j in range(3)
            ]
            for i in range(3)
        ]
        volume = deform[0][0] * cof[0][0] + deform[0][1] * cof[0][1] + deform[0][2] * cof[0][2]
        factor = bulk * (volume - 1.0) - shear
        piola = [[shear * deform[i][j] + factor * cof[i][j] for j in range(3)] for i in range(3)]
        for c in range(3):
            for i, value in (
                (c, back[0] * piola[c][0] + back[1] * piola[c][2]),
                (3 + c, back[2] * piola[c][0] + back[3] * piola[c][2]),
            ):
                v_hi, v_lo = split(value)
                parts[here, 128 * i : 128 * i + 128] = v_hi
                parts[here, 768 + 128 * i : 896 + 128 * i] = v_lo
        hoop = [weight * piola[c][1] for c in range(3)]
        for i, sense in ((0, 1.0), (1, -1.0)):
            pair = [jnp.where(plus, h + sense * turn(h, -NODES), 0.0) for h in hoop]
            first = 256 * i
            hoops[here, first : first + 128] = pair[1] - turn(pair[0], NODES)
            hoops[here, first + 128 : first + 256] = (
                pair[0] + turn(pair[1], NODES) + turn(pair[2], 2 * NODES)
            )
        return 0

    lax.fori_loop(0, HALF // STRIP, strip, 0, unroll=True)

    high, low = parts[:, 0:768], parts[:, 768:1536]
    b_hi, b_lo = block(9)
    straight = dot(high, b_hi) + dot(low, b_hi) + dot(high, b_lo)
    even = straight[:, 0:128] + hoops[:, 0:128]
    odd = straight[:, 128:256] + hoops[:, 256:384]
    half = ANGLES // 2
    for i, value in enumerate((even, hoops[:, 384:512], odd, hoops[:, 128:256])):
        v_hi, v_lo = split(value[0:half])
        sums[half * i : half * i + half, 0:128] = v_hi
        sums[half * i : half * i + half, 128:256] = v_lo

    step = 2.0 * math.pi / ANGLES
    row = lax.broadcasted_iota(jnp.int32, (MODES, 128), 0)
    signed = (0.5 * step) * (1.0 - 2.0 * (row % 2).astype(f32))
    weights = jnp.where(row == 0, 0.5 * signed, signed) * 2.0
    last = jnp.sum(weights * even[0:half], axis=0, keepdims=True) + 0.5 * step * even[half : half + 1]
    pieces = [(sums[half * i : half * i + half, 0:128], sums[half * i : half * i + half, 128:256]) for i in range(4)]
    cos_part = product(*block(2), *pieces[0]) + product(*block(3), *pieces[1])
    result[pl.ds(0, MODES, stride=2), :] = cos_part + signed * even[half : half + 1]
    sin_part = product(*block(4), *pieces[2]) + product(*block(5), *pieces[3])
    sin_part = sin_part + (row.astype(f32) * signed) * hoops[half : half + 1, 128:256]
    result[pl.ds(1, MODES, stride=2), :] = jnp.where(row == 0, last, sin_part)


def kernel(
    disp_in, metric_in, weight_in, radius_in, moduli_in, neigh_in, side_in, pres_in,
    table_in,
    out,
    disp, metric, weights, radii, moduli, neigh, side, pres,
    pack, got1, got2, state1, result, back0, back1, home0, home1, perm, rims, rims_back, rim_out, rim_in, base, traces, partial,
    even_odd, turns, grads, parts, hoops, sums,
    table,
    relay1, relay2, relay3, relay4,
    disp_sem, small_sem, table_sem,
    s1, r1, m1, o1, s2, r2, m2, o2, s3, r3, m3, o3, s4, r4, m4, o4,
    rim_send, rim_recv,
):
    sems1, sems2, sems3, sems4 = (s1, r1, m1, o1), (s2, r2, m2, o2), (s3, r3, m3, o3), (s4, r4, m4, o4)
    elem = lax.axis_index("elem")
    mode = lax.axis_index("mode")
    runs = lax.axis_size("elem")
    half, rest = mode // 8, mode % 8
    row, core = rest // 2, rest % 2
    height = half * 8 + elem // 4

    def place(dz, dy, dc):
        there = (height + dz + 16) % 16
        column = (row + dy + 4) % 4 * 2 + (core + dc + 2) % 2
        return there % 8 * 4 + elem % 4, there // 8 * 8 + column

    disp_copies = [pltpu.make_async_copy(disp_in.at[s], disp.at[s], disp_sem.at[s]) for s in range(2)]
    for copy in disp_copies:
        copy.start()
    barrier = pltpu.get_barrier_semaphore()
    senders = [place(-LEG * up, -dy, -dc) for dy, dc, up in CROSS] + [place(LEG, 0, 0)]
    senders += [place(0, -dy, -dc) for dy, dc in LOCAL]
    for sender in senders:
        pl.semaphore_signal(barrier, inc=1, device_id=sender, device_id_type=MESH)

    @pl.when(elem > 0)
    def _():
        pl.semaphore_signal(barrier, inc=1, device_id=(elem - 1, mode), device_id_type=MESH)

    @pl.when(elem < runs - 1)
    def _():
        pl.semaphore_signal(barrier, inc=1, device_id=(elem + 1, mode), device_id_type=MESH)

    small_copies = [
        pltpu.make_async_copy(src, dst, small_sem.at[i])
        for i, (src, dst) in enumerate(
            [(metric_in, metric), (weight_in, weights), (radius_in, radii), (moduli_in, moduli),
             (neigh_in, neigh), (side_in, side), (pres_in, pres)]
        )
    ]
    for copy in small_copies:
        copy.start()

    lane = lax.broadcasted_iota(jnp.int32, (OWN, 128), 1)
    lane8 = lax.broadcasted_iota(jnp.int32, (8, 128), 1)

    def column(s, c, g):
        if g < 4:
            return disp[s, c, :, 128 * g : 128 * g + 128]
        return jnp.concatenate([disp[s, c, :, 512:576], jnp.zeros((OWN, 64), f32)], axis=1)

    def gather_element(s, j, base_lane):
        result = jnp.zeros((OWN, 128), f32)
        for c in range(3):
            target = NODES * c + base_lane
            first = NODES * j
            for g in range(first // 128, (first + NODES - 1) // 128 + 1):
                low = max(first, 128 * g)
                high = min(first + NODES, 128 * g + 128)
                moved = turn(column(s, c, g), target - (first - 128 * g))
                begin = (target + low - first) % 128
                end = begin + high - low
                inside = (lane >= begin) & (lane < end)
                if end > 128:
                    inside = (lane >= begin) | (lane < end - 128)
                result = jnp.where(inside, moved, result)
        return result

    def pack_rows(full, ragged):
        last = ragged[24:32]
        tails = [turn(last, 88), turn(last, 48), turn(last, 8)]
        rows = [jnp.where(lane8 < 88, ragged[8 * t : 8 * t + 8], tails[t]) for t in range(3)]
        return jnp.where(lane < 108, full, ragged), jnp.concatenate(rows, axis=0)

    def unpack_ragged(first, second):
        rows = [
            jnp.where(lane8 < 88, second[8 * t : 8 * t + 8], first[8 * t : 8 * t + 8]) for t in range(3)
        ]
        moved = [turn(second[0:8], -88), turn(second[8:16], -48), turn(second[16:24], -8)]
        last = jnp.where(lane8 < 40, moved[0], jnp.where(lane8 < 80, moved[1], moved[2]))
        rows.append(jnp.where(lane8 < 88, last, first[24:32]))
        return jnp.concatenate(rows, axis=0)

    for copy in disp_copies:
        copy.wait()
    for j in range(PEERS):
        full = gather_element(0, j, 0)
        ragged = gather_element(1, j, 108)
        top, bottom = pack_rows(full, ragged)
        pack[j, 0:32, :] = top
        pack[j, 32:56, :] = bottom

    table_copy = pltpu.make_async_copy(table_in, table, table_sem)
    table_copy.start()

    neighbours_there = 2 - (elem == 0).astype(jnp.int32) - (elem == runs - 1).astype(jnp.int32)
    pl.semaphore_wait(barrier, len(senders) + neighbours_there)

    class Exchange:
        def __init__(self, source, target, arrivals, relay, sems):
            send, recv, relayed, onward = sems
            self.all = arrivals, relay, send, recv, onward
            self.first, self.second, self.local = [], [], []
            for i, (dy, dc, up) in enumerate(CROSS):
                owner = place(2 * LEG, dy, dc)[1]
                origin = place(-LEG * up, 0, 0)[1]
                self.first.append(
                    pltpu.make_async_remote_copy(
                        src_ref=source(owner), dst_ref=relay.at[i],
                        send_sem=send, recv_sem=relayed.at[i],
                        device_id=place(LEG * up, 0, 0), device_id_type=MESH,
                    )
                )
                self.second.append(
                    pltpu.make_async_remote_copy(
                        src_ref=relay.at[i], dst_ref=target(origin),
                        send_sem=onward, recv_sem=recv,
                        device_id=place(LEG * up, dy, dc), device_id_type=MESH,
                    )
                )
            for i, (dy, dc) in enumerate(LOCAL):
                to = place(0, dy, dc)
                self.local.append(
                    pltpu.make_async_remote_copy(
                        src_ref=source(to[1]), dst_ref=target(mode),
                        send_sem=send, recv_sem=recv,
                        device_id=to, device_id_type=MESH,
                    )
                )

        def start(self):
            for copy in self.first + self.local:
                copy.start()

        def forward(self):
            for first, second in zip(self.first, self.second):
                first.wait_recv()
                second.start()

        def arrive(self):
            arrivals, _, _, recv, _ = self.all
            pltpu.make_async_copy(arrivals, arrivals, recv).wait()

        def finish(self):
            arrivals, relay, send, _, onward = self.all
            pltpu.make_async_copy(arrivals, arrivals, send).wait()
            pltpu.make_async_copy(relay, relay, onward).wait()

    def full_rows(me):
        return got1.at[pl.ds(pl.multiple_of(me * OWN, OWN), OWN)]

    there1 = Exchange(lambda to: pack.at[to, 0:32], full_rows, got1.at[0 : 15 * OWN], relay1, sems1)
    there2 = Exchange(lambda to: pack.at[to, 32:56], lambda me: got2.at[me], got2.at[0:15], relay2, sems2)
    again0 = Exchange(lambda to: back0.at[to], lambda me: home0.at[me], home0.at[0:15], relay3, sems3)
    again1 = Exchange(lambda to: back1.at[to], lambda me: home1.at[me], home1.at[0:15], relay4, sems4)
    there1.start()
    there2.start()
    got1[pl.ds(pl.multiple_of(mode * OWN, OWN), OWN), :] = pack[mode, 0:32, :]
    got2[mode] = pack[mode, 32:56, :]

    for copy in small_copies:
        copy.wait()

    def wide(pieces):
        return jnp.concatenate(pieces + [jnp.zeros((1, WIDE - POINTS), f32)], axis=1)

    def as_row(ref):
        return wide([ref[128 * g : min(128 * g + 128, POINTS)].reshape(1, -1) for g in range(5)])

    geo = [wide([metric[i : i + 1, :]]) for i in range(4)] + [as_row(weights), as_row(radii)]
    stacked = jnp.concatenate(geo + [jnp.zeros((2, WIDE), f32)], axis=0)
    stacked = pltpu.roll(stacked, (WIDE - NODES * mode) % WIDE, 1)

    def own_row(i):
        return stacked[i : i + 1, 0:128]

    lane1 = lax.broadcasted_iota(jnp.int32, (1, 128), 1)
    own = [jnp.where(lane1 < NODES, own_row(i), 0.0) for i in range(6)]
    own = [r + turn(r, NODES) for r in own]
    own[5] = jnp.where(lane1 < 2 * NODES, own[5], 1.0)
    shear = moduli[0, mode]
    bulk = moduli[1, mode]

    first_elem = elem * PEERS
    head = jnp.int32(0)
    tail = jnp.int32(0)
    point = lax.broadcasted_iota(jnp.int32, (1, WIDE), 1)
    e_lane = sum((point >= NODES * i).astype(jnp.int32) for i in range(1, PEERS + 1))
    inner = point - NODES * e_lane
    a_lane = sum((inner >= 6 * i).astype(jnp.int32) for i in range(1, 6))
    b_lane = inner - 6 * a_lane
    partner = jnp.full((1, WIDE), -1, jnp.int32)
    sides = jnp.zeros((1, WIDE), jnp.int32)
    for e in range(PEERS):
        prev = neigh[0, e] - first_elem
        nxt = neigh[1, e] - first_elem
        prev_here = (prev >= 0) & (prev < PEERS)
        next_here = (nxt >= 0) & (nxt < PEERS)
        head = head + jnp.where(prev_here, 0, e)
        tail = tail + jnp.where(next_here, 0, e)
        low = jnp.where(prev_here, prev * NODES + 5, -10000)
        high = jnp.where(next_here, nxt * NODES, -10000)
        here = e_lane == e
        partner = jnp.where(here & (b_lane == 0), low + 6 * a_lane, partner)
        partner = jnp.where(here & (b_lane == 5), high + 6 * a_lane, partner)
        sides = jnp.where(here, side[e], sides)
    for g in range(5):
        rows = lax.broadcasted_iota(jnp.int32, (128, WIDE), 0) + 128 * g
        perm[128 * g : 128 * g + 128, :] = jnp.where(rows == partner, 1.0, 0.0).astype(bf16)
    slot = sum((lane1 >= 6 * i).astype(jnp.int32) for i in range(1, 13))
    node = lane1 - 6 * slot
    head_node = jnp.where(slot < 12, head * NODES + 6 * node, -1)
    tail_node = jnp.where(slot < 12, tail * NODES + 6 * node + 5, -1)
    for g in range(5):
        rows = lax.broadcasted_iota(jnp.int32, (128, 128), 0) + 128 * g
        rims[128 * g : 128 * g + 128, 0:128] = jnp.where(rows == head_node, 1.0, 0.0).astype(bf16)
        rims[128 * g : 128 * g + 128, 128:256] = jnp.where(rows == tail_node, 1.0, 0.0).astype(bf16)
    line = lax.broadcasted_iota(jnp.int32, (128, WIDE), 0)
    line_slot = sum((line >= 6 * i).astype(jnp.int32) for i in range(1, 13))
    line_node = 6 * (line - 6 * line_slot)
    line_used = line_slot < 12
    for way, first in ((0, head * NODES), (1, tail * NODES + 5)):
        match = line_used & (point == first + line_node)
        rims_back[128 * way : 128 * way + 128, :] = jnp.where(match, 1.0, 0.0).astype(bf16)
    facing = (a_lane == 5 * sides) & (e_lane < PEERS)
    outward = (2 * sides - 1).astype(f32)
    face = jnp.where(facing, 15.0 * outward * geo[4] * geo[5], 0.0)
    order = lax.broadcasted_iota(jnp.int32, (OWN, 128), 0)
    pressure = jnp.zeros((OWN, 128), f32)
    for i in range(OWN):
        pressure = jnp.where(order == i, pres[i], pressure)
    for g in range(5):
        columns = slice(128 * g, 128 * g + 128)
        base[0, :, columns] = pressure * (face * geo[0])[:, columns]
        base[1, :, columns] = pressure * (face * geo[1])[:, columns]

    table_copy.wait()

    scratch = (even_odd, turns, grads, parts, hoops, sums)

    there1.forward()
    there2.forward()
    there1.arrive()

    evaluate(got1, result, own, shear, bulk, table, scratch)
    for i in range(PEERS):
        block = turn(result[OWN * i : OWN * i + OWN, :], 108)
        _, bottom = pack_rows(block, block)
        back0[i] = bottom
        back1[i] = block
    again0.start()
    home0[mode] = back0[mode]

    there2.arrive()
    for i in range(PEERS):
        state1[OWN * i : OWN * i + OWN, :] = turn(unpack_ragged(got1[OWN * i : OWN * i + OWN, :], got2[i]), 20)

    evaluate(state1, result, own, shear, bulk, table, scratch)
    for i in range(PEERS):
        back1[i] = jnp.where(lane < 108, result[OWN * i : OWN * i + OWN, :], back1[i])
    again1.start()
    home1[mode] = back1[mode]

    again0.forward()
    again1.forward()
    def side_by_side(pieces, c):
        columns = []
        for g in range(5):
            acc = jnp.zeros((OWN, 128), f32)
            for i in range(PEERS):
                low = max(NODES * i, 128 * g) - 128 * g
                high = min(NODES * i + NODES, 128 * g + 128) - 128 * g
                if low < high:
                    moved = turn(pieces[i], NODES * i - 128 * g - NODES * c)
                    acc = jnp.where((lane >= low) & (lane < high), moved, acc)
            columns.append(acc)
        whole = jnp.concatenate(columns, axis=1)
        return whole if c == 1 else whole + base[c // 2]

    def assemble(first, l_hi, l_lo, loaded):
        rows = slice(first, first + loaded.shape[0])
        partial[rows, :] = loaded + dot(l_hi, perm[...]) + dot(l_lo, perm[...])

    def trace(first, l_hi, l_lo):
        rows = slice(first, first + l_hi.shape[0])
        traces[rows, :] = dot(l_hi, rims[...]) + dot(l_lo, rims[...])

    again0.arrive()
    early = [turn(unpack_ragged(back1[i], home0[i]), 20) for i in range(PEERS)]
    early = jnp.concatenate([side_by_side(early, 1), side_by_side(early, 2)], axis=0)
    early_parts = split(early)
    trace(0, *early_parts)
    assemble(0, *early_parts, early)
    again1.arrive()
    late = [turn(unpack_ragged(home1[i], home0[i]), 20) for i in range(PEERS)]
    late = [side_by_side(late, 0)] + [side_by_side([home1[i] for i in range(PEERS)], c) for c in range(3)]
    late = jnp.concatenate(late, axis=0)
    late_parts = split(late)
    trace(64, *late_parts)

    for way in range(2):
        columns = slice(128 * way, 128 * way + 128)
        for s in range(2):
            tile = jnp.zeros((8, 128), f32)
            for t in range(12):
                tile = jnp.where(slot == t, traces[96 * s + 8 * t : 96 * s + 8 * t + 8, columns], tile)
            rim_out[way, 8 * s : 8 * s + 8, :] = tile

    to_prev = pltpu.make_async_remote_copy(
        src_ref=rim_out.at[0], dst_ref=rim_in.at[1], send_sem=rim_send.at[0], recv_sem=rim_recv.at[1],
        device_id=(jnp.maximum(elem - 1, 0), mode), device_id_type=MESH,
    )
    to_next = pltpu.make_async_remote_copy(
        src_ref=rim_out.at[1], dst_ref=rim_in.at[0], send_sem=rim_send.at[1], recv_sem=rim_recv.at[0],
        device_id=(jnp.minimum(elem + 1, runs - 1), mode), device_id_type=MESH,
    )

    @pl.when(elem > 0)
    def _():
        to_prev.start()

    @pl.when(elem < runs - 1)
    def _():
        to_next.start()

    assemble(64, *late_parts, late)

    @pl.when(elem > 0)
    def _():
        to_next.wait_recv()

    @pl.when(elem < runs - 1)
    def _():
        to_prev.wait_recv()

    arrived = []
    for way, there in ((0, elem > 0), (1, elem < runs - 1)):
        rows = []
        for s in range(2):
            tile = jnp.where(there, rim_in[way, 8 * s : 8 * s + 8, :], 0.0)
            rows += [jnp.where(slot == t, tile, 0.0) for t in range(12)]
        arrived.append(jnp.concatenate(rows, axis=0))
    a_hi, a_lo = split(jnp.concatenate(arrived, axis=1))
    places = [(0, 1), (0, 2), (0, 0), (1, 0), (1, 1), (1, 2)]
    for s in range(2):
        half_rows = slice(96 * s, 96 * s + 96)
        block = partial[half_rows, :] + dot(a_hi[half_rows], rims_back[...]) + dot(a_lo[half_rows], rims_back[...])
        for i in range(3):
            out[places[3 * s + i]] = block[32 * i : 32 * i + 32, 0:POINTS]
    for exchange in (there1, there2, again0, again1):
        exchange.finish()

    @pl.when(elem > 0)
    def _():
        to_prev.wait_send()

    @pl.when(elem < runs - 1)
    def _():
        to_next.wait_send()


EVALUATE_SCRATCH = [
    pltpu.VMEM((HALF, 256), f32),
    pltpu.VMEM((HALF, 256), f32),
    pltpu.VMEM((HALF, 768), f32),
    pltpu.VMEM((HALF, 1536), bf16),
    pltpu.VMEM((HALF, 512), f32),
    pltpu.VMEM((2 * ANGLES, 256), bf16),
]


def on_device(displacement, metric, weight_jac, radius, moduli, neighbours, inner_side, pressure):
    table = jnp.asarray(tables())
    hbm, vmem = pl.BlockSpec(memory_space=pltpu.HBM), pl.BlockSpec(memory_space=pltpu.VMEM)
    single = pltpu.SemaphoreType.DMA
    sems = [single, single, pltpu.SemaphoreType.DMA((len(CROSS),)), single]
    return pl.pallas_call(
        kernel,
        out_shape=jax.ShapeDtypeStruct((2, 3, OWN, POINTS), f32),
        in_specs=[hbm] * 9,
        out_specs=vmem,
        scratch_shapes=[
            pltpu.VMEM((2, 3, OWN, POINTS), f32),
            pltpu.VMEM((4, POINTS), f32),
            pltpu.VMEM((POINTS,), f32),
            pltpu.VMEM((POINTS,), f32),
            pltpu.SMEM((2, PEERS), f32),
            pltpu.SMEM((2, PEERS), jnp.int32),
            pltpu.SMEM((PEERS,), jnp.int32),
            pltpu.SMEM((OWN,), f32),
            pltpu.VMEM((PEERS, 56, 128), f32),
            pltpu.VMEM((COEFS, 128), f32),
            pltpu.VMEM((PEERS, 24, 128), f32),
            pltpu.VMEM((COEFS, 128), f32),
            pltpu.VMEM((COEFS, 128), f32),
            pltpu.VMEM((PEERS, 24, 128), f32),
            pltpu.VMEM((PEERS, 32, 128), f32),
            pltpu.VMEM((PEERS, 24, 128), f32),
            pltpu.VMEM((PEERS, 32, 128), f32),
            pltpu.VMEM((WIDE, WIDE), bf16),
            pltpu.VMEM((WIDE, 256), bf16),
            pltpu.VMEM((256, WIDE), bf16),
            pltpu.VMEM((2, 16, 128), f32),
            pltpu.VMEM((2, 16, 128), f32),
            pltpu.VMEM((2, OWN, WIDE), f32),
            pltpu.VMEM((192, 256), f32),
            pltpu.VMEM((192, WIDE), f32),
            *EVALUATE_SCRATCH,
            pltpu.VMEM(table.shape, bf16),
            *[pltpu.VMEM((len(CROSS), n, 128), f32) for n in (32, 24, 24, 32)],
            pltpu.SemaphoreType.DMA((2,)),
            pltpu.SemaphoreType.DMA((7,)),
            pltpu.SemaphoreType.DMA,
            *sems * 4,
            pltpu.SemaphoreType.DMA((2,)),
            pltpu.SemaphoreType.DMA((2,)),
        ],
        compiler_params=pltpu.CompilerParams(
            collective_id=0, has_side_effects=True, vmem_limit_bytes=64 * 2**20
        ),
        name="bellows",
    )(
        displacement, metric, weight_jac, radius, moduli, neighbours.T, inner_side, pressure,
        table,
    )


def solution(mesh):
    placed = (
        P(None, None, "mode", "elem"),
        P(None, "elem"),
        P("elem"),
        P("elem"),
        P(None, "elem"),
        P("elem", None),
        P("elem"),
        P("mode"),
    )
    return jax.shard_map(
        on_device,
        mesh=mesh,
        in_specs=placed,
        out_specs=P(None, None, "mode", "elem"),
        check_vma=False,
    )
```

time: 84.5 us -> 71.8 us (0.85)
  the two profiles are of different devices: /device:TPU:64 before, /device:TPU:32 now
where the time goes in v1:
time: 71.8 us; the launch traced here: 71.6 us
  Pallas kernels  69.7 us (97%)
  local copies, waits for them, and re-layouts  1.84 us (3%)
    pallas_call x1, Pallas kernels, on_device(): pl.pallas_call(kernel, out_shape=jax.ShapeDtypeStruct((2, 3, OWN, POINTS)...  69.7 us
    unnamed x1, local copies, waits for them, and re-layouts  1.84 us

profile of v1, /device:TPU:32, one launch (start us, length us, event | category | flops | bytes accessed | tf_op | source)
XLA Modules:
  0.0 71.6 jit_solution(192336083752142762)
XLA Ops:
  0.0 69.7 %bellows.1 = f32[2,3,32,576]{3,2,1,0:T(8,128)} custom-call(f32[2,3,32,576]{3,2,1,0:T(8,128)} %disp_in.1, f32[4,576]{1,0:T(4,128)} %metric_in.1, f32[576]{0:T(1024)} %weight_in.1, f32[576]{0:T(1024)} %radius_in.1, f32[2,16]{1,0:T(2,128)} %moduli_in.1, s32[2,16]{1,0:T(2,128)} %bitcast.1, s32[16]{0:T(128)} %side_in.1, f32[32]{0:T(128)} %pres_in.1, ...), custom_call_target="tpu_custom_call" | custom-call | tf_op jit(solution)/shard_map/bellows/pallas_call | solution.py:587
  69.7 1.8 %copy.11 = f32[2,3,32,576]{3,2,1,0:T(8,128)} copy(f32[2,3,32,576]{3,2,1,0:T(8,128)} %bellows.1) | data formatting | bytes 884736

commit v2 on v1

--- a/solution.py
+++ b/solution.py
@@ -206,12 +206,12 @@
     pack, got1, got2, state1, result, back0, back1, home0, home1, perm, rims, rims_back, rim_out, rim_in, base, traces, partial,
     even_odd, turns, grads, parts, hoops, sums,
     table,
-    relay1, relay2, relay3, relay4,
+    relay1,
     disp_sem, small_sem, table_sem,
-    s1, r1, m1, o1, s2, r2, m2, o2, s3, r3, m3, o3, s4, r4, m4, o4,
+    s1, r1, m1, o1, s2, r2, s3, r3, s4, r4, far,
     rim_send, rim_recv,
 ):
-    sems1, sems2, sems3, sems4 = (s1, r1, m1, o1), (s2, r2, m2, o2), (s3, r3, m3, o3), (s4, r4, m4, o4)
+    sems1, sems2, sems3, sems4 = (s1, r1, m1, o1), (s2, r2, None, None), (s3, r3, None, None), (s4, r4, None, None)
     elem = lax.axis_index("elem")
     mode = lax.axis_index("mode")
     runs = lax.axis_size("elem")
@@ -307,43 +307,35 @@
     pl.semaphore_wait(barrier, len(senders) + neighbours_there)
 
     class Exchange:
-        def __init__(self, source, target, arrivals, relay, sems):
+        def __init__(self, source, target, arrivals, sems, relay=None):
             send, recv, relayed, onward = sems
             self.all = arrivals, relay, send, recv, onward
-            self.first, self.second, self.local = [], [], []
+            self.first, self.second = [], []
+
+            def copy(src, dst, sent, received, to):
+                return pltpu.make_async_remote_copy(
+                    src_ref=src, dst_ref=dst, send_sem=sent, recv_sem=received,
+                    device_id=to, device_id_type=MESH,
+                )
+
             for i, (dy, dc, up) in enumerate(CROSS):
-                owner = place(2 * LEG, dy, dc)[1]
+                owner = place(2 * LEG, dy, dc)
+                if relay is None:
+                    self.first.append(copy(source(owner[1]), target(mode), send, recv, owner))
+                    continue
                 origin = place(-LEG * up, 0, 0)[1]
-                self.first.append(
-                    pltpu.make_async_remote_copy(
-                        src_ref=source(owner), dst_ref=relay.at[i],
-                        send_sem=send, recv_sem=relayed.at[i],
-                        device_id=place(LEG * up, 0, 0), device_id_type=MESH,
-                    )
-                )
-                self.second.append(
-                    pltpu.make_async_remote_copy(
-                        src_ref=relay.at[i], dst_ref=target(origin),
-                        send_sem=onward, recv_sem=recv,
-                        device_id=place(LEG * up, dy, dc), device_id_type=MESH,
-                    )
-                )
-            for i, (dy, dc) in enumerate(LOCAL):
+                self.first.append(copy(source(owner[1]), relay.at[i], send, relayed.at[i], place(LEG * up, 0, 0)))
+                self.second.append(copy(relay.at[i], target(origin), onward, recv, place(LEG * up, dy, dc)))
+            for dy, dc in LOCAL:
                 to = place(0, dy, dc)
-                self.local.append(
-                    pltpu.make_async_remote_copy(
-                        src_ref=source(to[1]), dst_ref=target(mode),
-                        send_sem=send, recv_sem=recv,
-                        device_id=to, device_id_type=MESH,
-                    )
-                )
+                self.first.append(copy(source(to[1]), target(mode), send, recv, to))
 
         def start(self):
-            for copy in self.first + self.local:
-                copy.start()
-
-        def forward(self):
-            for first, second in zip(self.first, self.second):
+            for one in self.first:
+                one.start()
+
+        def forward(self, low=0, high=8):
+            for first, second in zip(self.first[low:high], self.second[low:high]):
                 first.wait_recv()
                 second.start()
 
@@ -354,17 +346,19 @@
         def finish(self):
             arrivals, relay, send, _, onward = self.all
             pltpu.make_async_copy(arrivals, arrivals, send).wait()
-            pltpu.make_async_copy(relay, relay, onward).wait()
+            if relay is not None:
+                pltpu.make_async_copy(relay, relay, onward).wait()
 
     def full_rows(me):
         return got1.at[pl.ds(pl.multiple_of(me * OWN, OWN), OWN)]
 
-    there1 = Exchange(lambda to: pack.at[to, 0:32], full_rows, got1.at[0 : 15 * OWN], relay1, sems1)
-    there2 = Exchange(lambda to: pack.at[to, 32:56], lambda me: got2.at[me], got2.at[0:15], relay2, sems2)
-    again0 = Exchange(lambda to: back0.at[to], lambda me: home0.at[me], home0.at[0:15], relay3, sems3)
-    again1 = Exchange(lambda to: back1.at[to], lambda me: home1.at[me], home1.at[0:15], relay4, sems4)
+    there1 = Exchange(lambda to: pack.at[to, 0:32], full_rows, got1.at[0 : 15 * OWN], sems1, relay1)
+    there2 = Exchange(lambda to: pack.at[to, 32:56], lambda me: got2.at[me], got2.at[0:15], sems2)
+    again0 = Exchange(lambda to: back0.at[to], lambda me: home0.at[me], home0.at[0:15], sems3)
+    again1 = Exchange(lambda to: back1.at[to], lambda me: home1.at[me], home1.at[0:15], sems4)
     there1.start()
-    there2.start()
+    for dz in (LEG, -LEG):
+        pl.semaphore_signal(far, inc=1, device_id=place(dz, 0, 0), device_id_type=MESH)
     got1[pl.ds(pl.multiple_of(mode * OWN, OWN), OWN), :] = pack[mode, 0:32, :]
     got2[mode] = pack[mode, 32:56, :]
 
@@ -448,8 +442,20 @@
 
     scratch = (even_odd, turns, grads, parts, hoops, sums)
 
-    there1.forward()
-    there2.forward()
+    there1.forward(0, 6)
+
+    @pl.when(half == 0)
+    def _():
+        pl.semaphore_wait(far, 2)
+        there2.start()
+
+    there1.forward(6, 8)
+
+    @pl.when(half == 1)
+    def _():
+        pl.semaphore_wait(far, 2)
+        there2.start()
+
     there1.arrive()
 
     evaluate(got1, result, own, shear, bulk, table, scratch)
@@ -471,8 +477,6 @@
     again1.start()
     home1[mode] = back1[mode]
 
-    again0.forward()
-    again1.forward()
     def side_by_side(pieces, c):
         columns = []
         for g in range(5):
@@ -583,7 +587,7 @@
     table = jnp.asarray(tables())
     hbm, vmem = pl.BlockSpec(memory_space=pltpu.HBM), pl.BlockSpec(memory_space=pltpu.VMEM)
     single = pltpu.SemaphoreType.DMA
-    sems = [single, single, pltpu.SemaphoreType.DMA((len(CROSS),)), single]
+    sems = [single, single, pltpu.SemaphoreType.DMA((len(CROSS),)), single] + [single] * 6
     return pl.pallas_call(
         kernel,
         out_shape=jax.ShapeDtypeStruct((2, 3, OWN, POINTS), f32),
@@ -617,11 +621,12 @@
             pltpu.VMEM((192, WIDE), f32),
             *EVALUATE_SCRATCH,
             pltpu.VMEM(table.shape, bf16),
-            *[pltpu.VMEM((len(CROSS), n, 128), f32) for n in (32, 24, 24, 32)],
+            pltpu.VMEM((len(CROSS), 32, 128), f32),
             pltpu.SemaphoreType.DMA((2,)),
             pltpu.SemaphoreType.DMA((7,)),
             pltpu.SemaphoreType.DMA,
-            *sems * 4,
+            *sems,
+            pltpu.SemaphoreType.REGULAR,
             pltpu.SemaphoreType.DMA((2,)),
             pltpu.SemaphoreType.DMA((2,)),
         ],

time: 71.8 us -> 70.3 us (0.979)
  the two profiles are of different devices: /device:TPU:32 before, /device:TPU:10 now
where the time goes in v2:
time: 70.3 us; the launch traced here: 70.1 us
  Pallas kernels  68.3 us (97%)
  local copies, waits for them, and re-layouts  1.84 us (3%)
    pallas_call x1, Pallas kernels, on_device(): pl.pallas_call(kernel, out_shape=jax.ShapeDtypeStruct((2, 3, OWN, POINTS)...  68.3 us
    unnamed x1, local copies, waits for them, and re-layouts  1.84 us

profile of v2, /device:TPU:10, one launch (start us, length us, event | category | flops | bytes accessed | tf_op | source)
XLA Modules:
  0.0 70.1 jit_solution(4714665768446513178)
XLA Ops:
  0.0 68.3 %bellows.1 = f32[2,3,32,576]{3,2,1,0:T(8,128)} custom-call(f32[2,3,32,576]{3,2,1,0:T(8,128)} %disp_in.1, f32[4,576]{1,0:T(4,128)} %metric_in.1, f32[576]{0:T(1024)} %weight_in.1, f32[576]{0:T(1024)} %radius_in.1, f32[2,16]{1,0:T(2,128)} %moduli_in.1, s32[2,16]{1,0:T(2,128)} %bitcast.1, s32[16]{0:T(128)} %side_in.1, f32[32]{0:T(128)} %pres_in.1, ...), custom_call_target="tpu_custom_call" | custom-call | tf_op jit(solution)/shard_map/bellows/pallas_call | solution.py:591
  68.3 1.8 %copy.11 = f32[2,3,32,576]{3,2,1,0:T(8,128)} copy(f32[2,3,32,576]{3,2,1,0:T(8,128)} %bellows.1) | data formatting | bytes 884736

commit v3 on v2

--- a/solution.py
+++ b/solution.py
@@ -442,14 +442,14 @@
 
     scratch = (even_odd, turns, grads, parts, hoops, sums)
 
-    there1.forward(0, 6)
+    there1.forward(0, 7)
 
     @pl.when(half == 0)
     def _():
         pl.semaphore_wait(far, 2)
         there2.start()
 
-    there1.forward(6, 8)
+    there1.forward(7, 8)
 
     @pl.when(half == 1)
     def _():

time: 70.3 us -> 69.2 us (0.984)
  the two profiles are of different devices: /device:TPU:10 before, /device:TPU:145 now
where the time goes in v3:
time: 69.2 us; the launch traced here: 69 us
  Pallas kernels  67.1 us (97%)
  local copies, waits for them, and re-layouts  1.84 us (3%)
    pallas_call x1, Pallas kernels, on_device(): pl.pallas_call(kernel, out_shape=jax.ShapeDtypeStruct((2, 3, OWN, POINTS)...  67.1 us
    unnamed x1, local copies, waits for them, and re-layouts  1.84 us

profile of v3, /device:TPU:145, one launch (start us, length us, event | category | flops | bytes accessed | tf_op | source)
XLA Modules:
  0.0 69.0 jit_solution(4593541238694196767)
XLA Ops:
  0.0 67.1 %bellows.1 = f32[2,3,32,576]{3,2,1,0:T(8,128)} custom-call(f32[2,3,32,576]{3,2,1,0:T(8,128)} %disp_in.1, f32[4,576]{1,0:T(4,128)} %metric_in.1, f32[576]{0:T(1024)} %weight_in.1, f32[576]{0:T(1024)} %radius_in.1, f32[2,16]{1,0:T(2,128)} %moduli_in.1, s32[2,16]{1,0:T(2,128)} %bitcast.1, s32[16]{0:T(128)} %side_in.1, f32[32]{0:T(128)} %pres_in.1, ...), custom_call_target="tpu_custom_call" | custom-call | tf_op jit(solution)/shard_map/bellows/pallas_call | solution.py:591
  67.2 1.8 %copy.11 = f32[2,3,32,576]{3,2,1,0:T(8,128)} copy(f32[2,3,32,576]{3,2,1,0:T(8,128)} %bellows.1) | data formatting | bytes 884736

commit v4 on v3

--- a/solution.py
+++ b/solution.py
@@ -203,7 +203,7 @@
     table_in,
     out,
     disp, metric, weights, radii, moduli, neigh, side, pres,
-    pack, got1, got2, state1, result, back0, back1, home0, home1, perm, rims, rims_back, rim_out, rim_in, base, traces, partial,
+    pack, got1, got2, state1, result, back0, back1, home0, home1, perm, rims, rims_back, rim_out, rim_in, base, traces, partial, final,
     even_odd, turns, grads, parts, hoops, sums,
     table,
     relay1,
@@ -555,12 +555,14 @@
             rows += [jnp.where(slot == t, tile, 0.0) for t in range(12)]
         arrived.append(jnp.concatenate(rows, axis=0))
     a_hi, a_lo = split(jnp.concatenate(arrived, axis=1))
+    out_copies = [pltpu.make_async_copy(final.at[s], out.at[s], disp_sem.at[s]) for s in range(2)]
     places = [(0, 1), (0, 2), (0, 0), (1, 0), (1, 1), (1, 2)]
     for s in range(2):
         half_rows = slice(96 * s, 96 * s + 96)
         block = partial[half_rows, :] + dot(a_hi[half_rows], rims_back[...]) + dot(a_lo[half_rows], rims_back[...])
         for i in range(3):
-            out[places[3 * s + i]] = block[32 * i : 32 * i + 32, 0:POINTS]
+            final[places[3 * s + i]] = block[32 * i : 32 * i + 32, 0:POINTS]
+        out_copies[s].start()
     for exchange in (there1, there2, again0, again1):
         exchange.finish()
 
@@ -571,6 +573,9 @@
     @pl.when(elem < runs - 1)
     def _():
         to_next.wait_send()
+
+    for copy in out_copies:
+        copy.wait()
 
 
 EVALUATE_SCRATCH = [
@@ -585,14 +590,14 @@
 
 def on_device(displacement, metric, weight_jac, radius, moduli, neighbours, inner_side, pressure):
     table = jnp.asarray(tables())
-    hbm, vmem = pl.BlockSpec(memory_space=pltpu.HBM), pl.BlockSpec(memory_space=pltpu.VMEM)
+    hbm = pl.BlockSpec(memory_space=pltpu.HBM)
     single = pltpu.SemaphoreType.DMA
     sems = [single, single, pltpu.SemaphoreType.DMA((len(CROSS),)), single] + [single] * 6
     return pl.pallas_call(
         kernel,
         out_shape=jax.ShapeDtypeStruct((2, 3, OWN, POINTS), f32),
         in_specs=[hbm] * 9,
-        out_specs=vmem,
+        out_specs=hbm,
         scratch_shapes=[
             pltpu.VMEM((2, 3, OWN, POINTS), f32),
             pltpu.VMEM((4, POINTS), f32),
@@ -619,6 +624,7 @@
             pltpu.VMEM((2, OWN, WIDE), f32),
             pltpu.VMEM((192, 256), f32),
             pltpu.VMEM((192, WIDE), f32),
+            pltpu.VMEM((2, 3, OWN, POINTS), f32),
             *EVALUATE_SCRATCH,
             pltpu.VMEM(table.shape, bf16),
             pltpu.VMEM((len(CROSS), 32, 128), f32),

time: 69.2 us -> 69.1 us (level)
  no operation moved by 1% of the time
where the time goes in v4:
time: 69.1 us; the launch traced here: 68.9 us
  Pallas kernels  67 us (97%)
  local copies, waits for them, and re-layouts  1.84 us (3%)
    pallas_call x1, Pallas kernels, on_device(): pl.pallas_call(kernel, out_shape=jax.ShapeDtypeStruct((2, 3, OWN, POINTS)...  67 us
    unnamed x1, local copies, waits for them, and re-layouts  1.84 us

profile of v4, /device:TPU:145, one launch (start us, length us, event | category | flops | bytes accessed | tf_op | source)
XLA Modules:
  0.0 68.9 jit_solution(6672593548873334323)
XLA Ops:
  0.0 67.0 %bellows.1 = f32[2,3,32,576]{3,2,1,0:T(8,128)} custom-call(f32[2,3,32,576]{3,2,1,0:T(8,128)} %disp_in.1, f32[4,576]{1,0:T(4,128)} %metric_in.1, f32[576]{0:T(1024)} %weight_in.1, f32[576]{0:T(1024)} %radius_in.1, f32[2,16]{1,0:T(2,128)} %moduli_in.1, s32[2,16]{1,0:T(2,128)} %bitcast.1, s32[16]{0:T(128)} %side_in.1, f32[32]{0:T(128)} %pres_in.1, ...), custom_call_target="tpu_custom_call" | custom-call | tf_op jit(solution)/shard_map/bellows/pallas_call | solution.py:596
  67.1 1.8 %copy.11 = f32[2,3,32,576]{3,2,1,0:T(8,128)} copy(f32[2,3,32,576]{3,2,1,0:T(8,128)} %bellows.1) | data formatting | bytes 884736
